TPU v7x, 32 devices: a whole 2x2x4 slice. The times are simulated.
32 devices in a mesh: snap: 2 (over y), row: 4 (over z), col: 4 (over x, core).
Axes of the slice: x: 2, y: 2, z: 4, core: 2. Of those that a mesh axis runs over, the one named last changes fastest.
Arguments:
- orbitals: float32 [12288, 768], P(('snap', 'row', 'col')), parts along dimension 0, may hold values from -6 to 6
- screened: float32 [6, 6144, 6144], P('snap', 'row', 'col'), parts along dimension 0, may hold values from -0.0029296875 to 0.0029296875
- green_weight: float32 [6, 768], P('snap'), parts along dimension 0, may hold values from 0.05 to 1
- time_weight: float32 [3], replicated, may hold values from 0.3 to 1
Outputs:
- updated: float32 [12288, 768], P(('snap', 'row', 'col')), parts along dimension 0
There are 2 independent parts, one for each index of `snap`. A program takes and returns all parts, laid end to end along the dimension named above; an argument that names none is the same for every part. Nothing has to cross between parts.
All inputs are finite; a program needn't handle non-finite values.
Results may differ from a plain program's by a relative error of at most 0.00013.
Values sent between devices are 32-bit elements; how exact they have to be, the bound alone decides.
No kernel may reach another device: no remote copies, remote signals or barrier semaphores. Data moves between devices by JAX's collectives and lax.ppermute only.
A program may use at most 128 MiB of HBM per device.

v0:
```python
import jax
import jax.numpy as jnp
from jax import lax
from jax.sharding import PartitionSpec as P

TIMES = 3
PASSES = 2


def from_root(block, axis, owner):
    block = jnp.where(lax.axis_index(axis) == owner, block, jnp.zeros_like(block))
    return lax.psum(block, axis)


def gather_rows(shard):
    return lax.all_gather(shard, "col", axis=0, tiled=True)


def scatter_rows(partial_value):
    return lax.psum_scatter(partial_value, "col", scatter_dimension=0, tiled=True)


def body(orbitals, screened, green_weight, time_weight):
    n_row = lax.axis_size("row")
    n_col = lax.axis_size("col")
    factor = n_col // n_row
    col_width = screened.shape[2]
    col_index = lax.axis_index("col")
    root = col_index // factor
    offset = col_index % factor * col_width
    own = orbitals
    rows = gather_rows(own)
    for step in range(PASSES):
        piece = lax.dynamic_slice_in_dim(rows, offset, col_width, 0)
        columns = from_root(piece, "row", root)
        partial_value = jnp.zeros(rows.shape, jnp.float32)
        for t in range(TIMES):
            green = lax.dot_general(
                rows * green_weight[t],
                columns,
                (((1,), (1,)), ((), ())),
                precision=lax.Precision.HIGHEST,
                preferred_element_type=jnp.float32,
            )
            applied = jnp.dot(
                green * screened[t],
                columns,
                precision=lax.Precision.HIGHEST,
                preferred_element_type=jnp.float32,
            )
            partial_value = partial_value + time_weight[t] * applied
        final = step == PASSES - 1
        own = own - scatter_rows(partial_value)
        if not final:
            rows = gather_rows(own)
    return own


def solution(mesh):
    in_specs = (P(("snap", "row", "col"), None), P("snap", "row", "col"), P("snap", None), P())
    out_specs = P(("snap", "row", "col"), None)
    return jax.shard_map(body, mesh=mesh, in_specs=in_specs, out_specs=out_specs, check_vma=False)
```

profile of v0, /device:TPU:0, one launch (start us, length us, event | category | flops | bytes accessed | tf_op | source)
XLA Modules:
  0.0 877.7 jit_solution(2341078948588468849)
XLA Ops:
  6.5 0.0 all-gather.3.cloned.1.call-start
  6.5 0.7 all-gather.3.cloned.1.call-update
  7.3 0.0 all-reduce.3.cloned.1.call-start
  7.3 41.8 %all-gather.3.cloned.1.call-done = f32[1536,768]{1,0:T(8,128)} async-done(((f32[384,768]{1,0:T(8,128)}), f32[1536,768]{1,0:T(8,128)}) %all-gather.3.cloned.1.call-update) | async-done | bytes 4718608 | tf_op jit(solution)/shard_map/all_gather | solution.py:16
  49.1 4.8 broadcast_select_fusion.1
  53.9 0.0 copy-start.4
  53.9 0.0 copy-start.3
  53.9 0.0 slice-start.7
  53.9 0.0 all-reduce.3.cloned.1.call-update
  53.9 0.0 reduce-scatter.3.cloned.1.call-start
  54.0 0.6 copy-done.4
  54.5 0.6 fusion.12
  55.2 0.0 copy-done.3
  55.2 170.7 %all-reduce.3.cloned.1.call-done = f32[1536,768]{1,0:T(8,128)} async-done(((f32[1536,768]{1,0:T(8,128)}), f32[1536,768]{1,0:T(8,128)}) %all-reduce.3.cloned.1.call-update) | async-done | bytes 4718608 | tf_op jit(solution)/shard_map/psum | solution.py:12
  225.9 0.0 slice-start
  225.9 0.0 slice-start.1
  225.9 0.0 slice-start.2
  225.9 0.0 slice-start.3
  225.9 0.0 slice-start.8
  225.9 28.3 %convolution_multiply_fusion.4 = f32[1536,1536]{1,0:T(8,128)} fusion(f32[1536,768]{1,0:T(8,128)} %all-reduce.3.cloned.1.call-done, f32[3,1536,1536]{2,1,0:T(8,128)} %param.5, f32[1536,768]{1,0:T(8,128)} %all-gather.3.cloned.1.call-done, f32[768]{0:T(1024)S(1)} %get-tuple-element.7), kind=kOutput, calls=%fused_computation.4 | convolution fusion | flops 21746810880 | bytes 28314624 | tf_op jit(solution)/shard_map/dot_general | solution.py:38
  254.2 0.0 slice-start.4
  254.2 0.0 slice-start.5
  254.2 0.0 slice-start.6
  254.2 28.0 %fusion.14 = f32[1536,768]{1,0:T(8,128)} fusion(f32[1536,1536]{1,0:T(8,128)} %convolution_multiply_fusion.4, f32[1536,768]{1,0:T(8,128)} %all-reduce.3.cloned.1.call-done), kind=kOutput, calls=%fused_computation.27 | convolution fusion | flops 21743271936 | bytes 18874368 | tf_op jit(solution)/shard_map/dot_general | solution.py:45
  282.2 0.0 slice-done.7
  282.2 0.0 slice-done
  282.2 0.0 slice-done.1
  282.2 0.0 slice-done.2
  282.2 0.0 slice-done.3
  282.2 0.0 slice-done.8
  282.2 0.0 slice-done.4
  282.3 0.0 slice-done.5
  282.3 0.0 slice-done.6
  282.3 26.8 %convolution_multiply_fusion.5 = f32[1536,1536]{1,0:T(8,128)} fusion(f32[1536,768]{1,0:T(8,128)} %all-reduce.3.cloned.1.call-done, f32[3,1536,1536]{2,1,0:T(8,128)S(1)} %bitcast.31, f32[1536,768]{1,0:T(8,128)S(1)} %bitcast.33, f32[768]{0:T(1024)S(1)} %get-tuple-element.6), kind=kOutput, calls=%fused_computation.5 | convolution fusion | flops 21746810880 | bytes 28314624 | tf_op jit(solution)/shard_map/dot_general | solution.py:38
  309.1 27.7 %fusion.13 = f32[1536,768]{1,0:T(8,128)} fusion(f32[1536,1536]{1,0:T(8,128)} %convolution_multiply_fusion.5, f32[1536,768]{1,0:T(8,128)} %all-reduce.3.cloned.1.call-done), kind=kOutput, calls=%fused_computation.26 | convolution fusion | flops 21743271936 | bytes 18874368 | tf_op jit(solution)/shard_map/dot_general | solution.py:45
  336.8 27.0 %convolution_multiply_fusion.3 = f32[1536,1536]{1,0:T(8,128)} fusion(f32[1536,768]{1,0:T(8,128)} %all-reduce.3.cloned.1.call-done, f32[3,1536,1536]{2,1,0:T(8,128)S(1)} %bitcast.31, f32[1536,768]{1,0:T(8,128)S(1)} %bitcast.33, f32[768]{0:T(1024)S(1)} %get-tuple-element.5), kind=kOutput, calls=%fused_computation.3 | convolution fusion | flops 21746810880 | bytes 28314624 | tf_op jit(solution)/shard_map/dot_general | solution.py:38
  363.8 31.6 %multiply_add_fusion.1 = f32[1536,768]{1,0:T(8,128)} fusion(f32[1536,768]{1,0:T(8,128)} %fusion.14, f32[1536,768]{1,0:T(8,128)} %fusion.13, f32[1536,1536]{1,0:T(8,128)} %convolution_multiply_fusion.3, f32[1536,768]{1,0:T(8,128)} %all-reduce.3.cloned.1.call-done, f32[]{:T(128)} %bitcast.4, f32[]{:T(128)} %bitcast.2, f32[]{:T(128)} %bitcast), kind=kOutput, calls=%fused_computation.10 | convolution fusion | flops 21749170176 | bytes 28311564 | tf_op jit(solution)/shard_map/dot_general | solution.py:45
  395.4 0.0 copy-start.2
  395.4 0.0 reduce-scatter.3.cloned.1.call-update
  395.5 0.0 all-gather.5.cloned.1.call-start
  395.5 46.9 %reduce-scatter.3.cloned.1.call-done = f32[384,768]{1,0:T(8,128)} async-done(((f32[1536,768]{1,0:T(8,128)}), f32[384,768]{1,0:T(8,128)}) %reduce-scatter.3.cloned.1.call-update) | async-done | bytes 1179664 | tf_op jit(solution)/shard_map/reduce_scatter | solution.py:20
  442.4 0.0 copy-done.2
  442.4 2.4 sub.8
  444.9 0.0 all-gather.5.cloned.1.call-update
  444.9 0.0 all-reduce.5.cloned.1.call-start
  444.9 37.6 %all-gather.5.cloned.1.call-done = f32[1536,768]{1,0:T(8,128)} async-done(((f32[384,768]{1,0:T(8,128)}), f32[1536,768]{1,0:T(8,128)}) %all-gather.5.cloned.1.call-update) | async-done | bytes 4718608 | tf_op jit(solution)/shard_map/all_gather | solution.py:16
  482.5 4.8 broadcast_select_fusion
  487.4 0.0 all-reduce.5.cloned.1.call-update
  487.4 0.0 reduce-scatter.5.cloned.1.call-start
  487.4 171.9 %all-reduce.5.cloned.1.call-done = f32[1536,768]{1,0:T(8,128)} async-done(((f32[1536,768]{1,0:T(8,128)}), f32[1536,768]{1,0:T(8,128)}) %all-reduce.5.cloned.1.call-update) | async-done | bytes 4718608 | tf_op jit(solution)/shard_map/psum | solution.py:12
  659.4 27.4 %convolution_multiply_fusion.1 = f32[1536,1536]{1,0:T(8,128)S(1)} fusion(f32[1536,768]{1,0:T(8,128)} %all-reduce.5.cloned.1.call-done, f32[3,1536,1536]{2,1,0:T(8,128)} %param.5, f32[1536,768]{1,0:T(8,128)} %all-gather.5.cloned.1.call-done, f32[768]{0:T(1024)S(1)} %get-tuple-element.7), kind=kOutput, calls=%fused_computation.1 | convolution fusion | flops 21746810880 | bytes 28314624 | tf_op jit(solution)/shard_map/dot_general | solution.py:38
  686.8 0.0 copy-done
  686.8 0.0 slice-start.10
  686.8 27.3 %convolution_multiply_fusion.2 = f32[1536,1536]{1,0:T(8,128)} fusion(f32[1536,768]{1,0:T(8,128)S(1)} %copy-done, f32[3,1536,1536]{2,1,0:T(8,128)} %param.5, f32[1536,768]{1,0:T(8,128)} %all-gather.5.cloned.1.call-done, f32[768]{0:T(1024)S(1)} %get-tuple-element.6), kind=kOutput, calls=%fused_computation.2 | convolution fusion | flops 21746810880 | bytes 28314624 | tf_op jit(solution)/shard_map/dot_general | solution.py:38
  714.2 0.0 slice-done.9
  714.2 0.0 slice-done.10
  714.2 28.4 %convolution_multiply_fusion = f32[1536,1536]{1,0:T(8,128)S(1)} fusion(f32[1536,768]{1,0:T(8,128)S(1)} %copy-done, f32[3,1536,1536]{2,1,0:T(8,128)} %param.5, f32[1536,768]{1,0:T(8,128)S(1)} %bitcast.35, f32[768]{0:T(1024)S(1)} %get-tuple-element.5), kind=kOutput, calls=%fused_computation | convolution fusion | flops 21746810880 | bytes 28314624 | tf_op jit(solution)/shard_map/dot_general | solution.py:38
  742.6 23.3 %fusion.16 = f32[1536,768]{1,0:T(8,128)S(1)} fusion(f32[1536,1536]{1,0:T(8,128)S(1)} %convolution_multiply_fusion.1, f32[1536,768]{1,0:T(8,128)S(1)} %copy-done), kind=kOutput, calls=%fused_computation.29 | convolution fusion | flops 21743271936 | bytes 18874368 | tf_op jit(solution)/shard_map/dot_general | solution.py:45
  765.9 28.4 %fusion.15 = f32[1536,768]{1,0:T(8,128)S(1)} fusion(f32[1536,1536]{1,0:T(8,128)} %convolution_multiply_fusion.2, f32[1536,768]{1,0:T(8,128)S(1)} %copy-done), kind=kOutput, calls=%fused_computation.28 | convolution fusion | flops 21743271936 | bytes 18874368 | tf_op jit(solution)/shard_map/dot_general | solution.py:45
  794.2 27.0 %multiply_add_fusion = f32[1536,768]{1,0:T(8,128)} fusion(f32[1536,768]{1,0:T(8,128)S(1)} %fusion.16, f32[1536,768]{1,0:T(8,128)S(1)} %fusion.15, f32[1536,1536]{1,0:T(8,128)S(1)} %convolution_multiply_fusion, f32[1536,768]{1,0:T(8,128)S(1)} %copy-done, f32[]{:T(128)} %bitcast.4, f32[]{:T(128)} %bitcast.2, f32[]{:T(128)} %bitcast), kind=kOutput, calls=%fused_computation.6 | convolution fusion | flops 21749170176 | bytes 28311564 | tf_op jit(solution)/shard_map/dot_general | solution.py:45
  821.2 0.0 reduce-scatter.5.cloned.1.call-update
  821.3 47.0 %reduce-scatter.5.cloned.1.call-done = f32[384,768]{1,0:T(8,128)} async-done(((f32[1536,768]{1,0:T(8,128)}), f32[384,768]{1,0:T(8,128)}) %reduce-scatter.5.cloned.1.call-update) | async-done | bytes 1179664 | tf_op jit(solution)/shard_map/reduce_scatter | solution.py:20
  868.2 0.0 copy-done.1
  868.2 2.4 sub.9
  (7 shorter events, 0.0 us)
Async XLA Ops:
  6.5 42.6 %all-gather.3.cloned.1.call-start = ((), (), s32[]{:S(2)}) async-start(), calls=%async_computation.2 | async-start | bytes 5898240 | tf_op jit(solution)/shard_map/all_gather | solution.py:16
  7.3 218.7 %all-reduce.3.cloned.1.call-start = ((), (), s32[]{:S(2)}) async-start(), calls=%async_computation.3 | async-start | bytes 9437184 | tf_op jit(solution)/shard_map/psum | solution.py:12
  53.9 0.7 copy-start.4
  53.9 1.3 copy-start.3
  53.9 228.3 %slice-start.7 = ((s8[4718592]{0:T(1024)(128)(4,1)}), s8[524288]{0:T(1024)(128)(4,1)S(1)}, s32[]{:S(2)}) async-start(s8[4718592]{0:T(1024)(128)(4,1)} %bitcast.32), calls=%async_computation.15 | async-start | bytes 1048576
  53.9 388.5 %reduce-scatter.3.cloned.1.call-start = ((), (), s32[]{:S(2)}) async-start(), calls=%async_computation.4 | async-start | bytes 5898240 | tf_op jit(solution)/shard_map/reduce_scatter | solution.py:20
  225.9 56.3 %slice-start = ((s8[28311552]{0:T(1024)(128)(4,1)}), s8[4194304]{0:T(1024)(128)(4,1)S(1)}, s32[]{:S(2)}) async-start(s8[28311552]{0:T(1024)(128)(4,1)} %bitcast.30), calls=%async_computation.8 | async-start | bytes 8388608
  225.9 56.3 %slice-start.1 = ((s8[28311552]{0:T(1024)(128)(4,1)}), s8[4194304]{0:T(1024)(128)(4,1)S(1)}, s32[]{:S(2)}) async-start(s8[28311552]{0:T(1024)(128)(4,1)} %bitcast.30), calls=%async_computation.9 | async-start | bytes 8388608
  225.9 56.3 %slice-start.2 = ((s8[28311552]{0:T(1024)(128)(4,1)}), s8[4194304]{0:T(1024)(128)(4,1)S(1)}, s32[]{:S(2)}) async-start(s8[28311552]{0:T(1024)(128)(4,1)} %bitcast.30), calls=%async_computation.10 | async-start | bytes 8388608
  225.9 56.3 %slice-start.3 = ((s8[28311552]{0:T(1024)(128)(4,1)}), s8[4194304]{0:T(1024)(128)(4,1)S(1)}, s32[]{:S(2)}) async-start(s8[28311552]{0:T(1024)(128)(4,1)} %bitcast.30), calls=%async_computation.11 | async-start | bytes 8388608
  225.9 56.3 %slice-start.8 = ((s8[4718592]{0:T(1024)(128)(4,1)}), s8[4194304]{0:T(1024)(128)(4,1)S(1)}, s32[]{:S(2)}) async-start(s8[4718592]{0:T(1024)(128)(4,1)} %bitcast.32), calls=%async_computation.16 | async-start | bytes 8388608
  254.2 28.0 %slice-start.4 = ((s8[28311552]{0:T(1024)(128)(4,1)}), s8[4194304]{0:T(1024)(128)(4,1)S(1)}, s32[]{:S(2)}) async-start(s8[28311552]{0:T(1024)(128)(4,1)} %bitcast.30), calls=%async_computation.12 | async-start | bytes 8388608
  254.2 28.1 %slice-start.5 = ((s8[28311552]{0:T(1024)(128)(4,1)}), s8[4194304]{0:T(1024)(128)(4,1)S(1)}, s32[]{:S(2)}) async-start(s8[28311552]{0:T(1024)(128)(4,1)} %bitcast.30), calls=%async_computation.13 | async-start | bytes 8388608
  254.2 28.1 %slice-start.6 = ((s8[28311552]{0:T(1024)(128)(4,1)}), s8[3145728]{0:T(1024)(128)(4,1)S(1)}, s32[]{:S(2)}) async-start(s8[28311552]{0:T(1024)(128)(4,1)} %bitcast.30), calls=%async_computation.14 | async-start | bytes 6291456
  395.4 47.0 %copy-start.2 = (f32[384,768]{1,0:T(8,128)S(1)}, f32[384,768]{1,0:T(8,128)}, u32[]{:S(2)}) copy-start(f32[384,768]{1,0:T(8,128)} %param.4) | copy-start | bytes 3538948
  395.5 87.1 %all-gather.5.cloned.1.call-start = ((), (), s32[]{:S(2)}) async-start(), calls=%async_computation.5 | async-start | bytes 5898240 | tf_op jit(solution)/shard_map/all_gather | solution.py:16
  444.9 214.5 %all-reduce.5.cloned.1.call-start = ((), (), s32[]{:S(2)}) async-start(), calls=%async_computation.6 | async-start | bytes 9437184 | tf_op jit(solution)/shard_map/psum | solution.py:12
  487.4 380.8 %reduce-scatter.5.cloned.1.call-start = ((), (), s32[]{:S(2)}) async-start(), calls=%async_computation.7 | async-start | bytes 5898240 | tf_op jit(solution)/shard_map/reduce_scatter | solution.py:20
  659.4 27.4 %copy-start = (f32[1536,768]{1,0:T(8,128)S(1)}, f32[1536,768]{1,0:T(8,128)}, u32[]{:S(2)}) copy-start(f32[1536,768]{1,0:T(8,128)} %all-reduce.5.cloned.1.call-done) | copy-start | bytes 14155780
  659.4 54.8 %slice-start.9 = ((s8[4718592]{0:T(1024)(128)(4,1)}), s8[4194304]{0:T(1024)(128)(4,1)S(1)}, s32[]{:S(2)}) async-start(s8[4718592]{0:T(1024)(128)(4,1)} %bitcast.34), calls=%async_computation.17 | async-start | bytes 8388608
  686.8 27.3 %slice-start.10 = ((s8[4718592]{0:T(1024)(128)(4,1)}), s8[524288]{0:T(1024)(128)(4,1)S(1)}, s32[]{:S(2)}) async-start(s8[4718592]{0:T(1024)(128)(4,1)} %bitcast.34), calls=%async_computation.18 | async-start | bytes 1048576
  821.2 47.0 %copy-start.1 = (f32[384,768]{1,0:T(8,128)S(1)}, f32[384,768]{1,0:T(8,128)}, u32[]{:S(2)}) copy-start(f32[384,768]{1,0:T(8,128)} %sub.8) | copy-start | bytes 3538948
Sparse Core Ops, SparseCore 0:
  8.9 40.1 all-gather.2
  54.0 171.8 all-reduce.2
  395.6 46.8 reduce-scatter.2
  445.0 37.4 all-gather.4
  487.5 171.8 all-reduce.4
  821.4 46.8 reduce-scatter.4
where the time goes:
time: 886 us; the launch traced here: 878 us
  waiting for transfers between devices  517 us (58%)
  matrix products  331 us (37%)
  other arithmetic  14.5 us (2%)
  between operations  13.9 us (2%)
    psum x2, waiting for transfers between devices, from_root(): return lax.psum(block, axis)  343 us
    dot_general x6, matrix products, body(): jnp.dot(green * screened[t], columns, precision=lax.Precision.HIGHEST, pr...  166 us
    dot_general x6, matrix products, body(): lax.dot_general(rows * green_weight[t], columns, (((1,), (1,)), ((), ()))...  165 us
    reduce_scatter x2, waiting for transfers between devices, scatter_rows(): lax.psum_scatter(partial_value, 'col', scatter_dimension=0, tiled=True)  93.9 us
    all_gather x2, waiting for transfers between devices, gather_rows(): return lax.all_gather(shard, 'col', axis=0, tiled=True)  79.4 us
  transfers between devices with their start and end apart: 6, of which 6 were waited for; matrix products, arithmetic and copies ran while one was open for 0% of the time, Pallas kernels for 0%

commit v1 on v0

v1 whole, which is shorter than its diff:
```python
import functools

import jax
import jax.numpy as jnp
from jax import lax
from jax.experimental import pallas as pl
from jax.experimental.pallas import tpu as pltpu
from jax.sharding import PartitionSpec as P

PASSES = 2
VMEM_BYTES = 60 * 2**20


def dot_t(a, b):
    return lax.dot_general(a, b, (((1,), (1,)), ((), ())), preferred_element_type=jnp.float32)


def dot_n(a, b):
    return lax.dot_general(a, b, (((1,), (0,)), ((), ())), preferred_element_type=jnp.float32)


def split(x):
    high = x.astype(jnp.bfloat16)
    return high, (x - high.astype(jnp.float32)).astype(jnp.bfloat16)


def apply_kernel(first, place, rows_ref, cols_ref, weight_ref, screened_ref, *rest):
    if first:
        out_ref, wh_ref, wl_ref, ch_ref, cl_ref = rest
    else:
        in_ref, out_ref, wh_ref, wl_ref, ch_ref, cl_ref = rest
    times = weight_ref.shape[0]

    @pl.when(pl.program_id(0) == 0)
    def _():
        cols = cols_ref[...]
        ch_ref[...], cl_ref[...] = split(cols)
        for t in range(times):
            wh_ref[t], wl_ref[t] = split(cols * weight_ref[t, :][None, :])

    high, low = split(rows_ref[...])
    mixed = None
    for t in range(times):
        green = dot_t(high, wh_ref[t]) + (dot_t(high, wl_ref[t]) + dot_t(low, wh_ref[t]))
        term = green * screened_ref[t]
        mixed = term if mixed is None else mixed + term
    high, low = split(mixed)
    applied = dot_n(high, ch_ref[...]) + (dot_n(high, cl_ref[...]) + dot_n(low, ch_ref[...]))
    out_ref[...] = applied if first else in_ref[...] + applied


def apply_chunk(place, rows, cols, weight, screened, partial_value, tile):
    n_rows, orbitals = rows.shape
    width = cols.shape[0]
    times = weight.shape[0]
    first = partial_value is None
    tile_spec = pl.BlockSpec((tile, orbitals), lambda i, place: (i, 0))
    in_specs = [
        tile_spec,
        pl.BlockSpec((width, orbitals), lambda i, place: (0, 0)),
        pl.BlockSpec((times, orbitals), lambda i, place: (0, 0)),
        pl.BlockSpec((times, tile, width), lambda i, place: (0, place[i], place[n_rows // tile])),
    ]
    args = [rows, cols, weight, screened]
    if not first:
        in_specs.append(tile_spec)
        args.append(partial_value)
    flops = 2 * n_rows * width * orbitals * 3 * (times + 1)
    return pl.pallas_call(
        functools.partial(apply_kernel, first),
        grid_spec=pltpu.PrefetchScalarGridSpec(
            num_scalar_prefetch=1,
            grid=(n_rows // tile,),
            in_specs=in_specs,
            out_specs=tile_spec,
            scratch_shapes=[
                pltpu.VMEM((times, width, orbitals), jnp.bfloat16),
                pltpu.VMEM((times, width, orbitals), jnp.bfloat16),
                pltpu.VMEM((width, orbitals), jnp.bfloat16),
                pltpu.VMEM((width, orbitals), jnp.bfloat16),
            ],
        ),
        out_shape=jax.ShapeDtypeStruct((n_rows, orbitals), jnp.float32),
        input_output_aliases={} if first else {5: 0},
        compiler_params=pltpu.CompilerParams(vmem_limit_bytes=VMEM_BYTES),
        cost_estimate=pl.CostEstimate(
            flops=flops,
            bytes_accessed=4 * (3 * n_rows * orbitals + times * n_rows * width),
            transcendentals=0,
        ),
        name="apply_chunk",
    )(place, *args)


def swap(value, bit, n_col):
    return lax.ppermute(value, "col", [(i, i ^ bit) for i in range(n_col)])


def gather_relative(own, n_col):
    shards = {0: own}
    bit = n_col // 2
    while bit:
        held = dict(shards)
        for p, shard in held.items():
            shards[p ^ bit] = swap(shard, bit, n_col)
        bit //= 2
    return [shards[p] for p in range(n_col)]


def scatter_relative(parts, n_col):
    bit = 1
    held = dict(enumerate(parts))
    while bit < n_col:
        held = {p: held[p] + swap(held[p ^ bit], bit, n_col) for p in held if not p & bit}
        bit *= 2
    return held[0]


def spread(chunk, n_row, n_col):
    factor = n_col // n_row
    root = lax.axis_index("col") // factor
    total = jnp.where(lax.axis_index("row") == root, chunk, jnp.zeros_like(chunk))
    for way in (1, -1):
        moving = chunk
        for hop in range(n_row - 1):
            pairs = []
            for c in range(n_col):
                at = c // factor + way * hop
                to = at + way
                if 0 <= at < n_row and 0 <= to < n_row:
                    pairs.append((at * n_col + c, to * n_col + c))
            moving = lax.ppermute(moving, ("row", "col"), pairs)
            total = total + moving
    return total


def body(orbitals, screened, green_weight, time_weight):
    n_row = lax.axis_size("row")
    n_col = lax.axis_size("col")
    factor = n_col // n_row
    shard = orbitals.shape[0]
    col_index = lax.axis_index("col")
    weight = green_weight * time_weight[:, None]
    own = orbitals
    fine = factor == 1 and shard % 128 == 0
    for step in range(PASSES):
        if fine:
            shards = gather_relative(own, n_col)
            rows = jnp.concatenate(shards, axis=0)
            row_place = [col_index ^ p for p in range(n_col)]
            partial_value = None
            for q in range(n_col):
                cols = spread(shards[q], n_row, n_col)
                place = jnp.stack(row_place + [col_index ^ q]).astype(jnp.int32)
                partial_value = apply_chunk(place, rows, cols, weight, screened, partial_value, shard)
            parts = [partial_value[p * shard : (p + 1) * shard] for p in range(n_col)]
            own = own - scatter_relative(parts, n_col)
        else:
            rows = lax.all_gather(own, "col", axis=0, tiled=True)
            width = screened.shape[2]
            piece = lax.dynamic_slice_in_dim(rows, col_index % factor * width, width, 0)
            cols = spread(piece, n_row, n_col)
            tile = 8 * max(d for d in range(1, 33) if rows.shape[0] % (8 * d) == 0)
            place = jnp.arange(rows.shape[0] // tile + 1, dtype=jnp.int32) % (rows.shape[0] // tile)
            partial_value = apply_chunk(place, rows, cols, weight, screened, None, tile)
            own = own - lax.psum_scatter(partial_value, "col", scatter_dimension=0, tiled=True)
    return own


def solution(mesh):
    in_specs = (P(("snap", "row", "col"), None), P("snap", "row", "col"), P("snap", None), P())
    out_specs = P(("snap", "row", "col"), None)
    return jax.shard_map(body, mesh=mesh, in_specs=in_specs, out_specs=out_specs, check_vma=False)
```

time: 886 us -> 534 us (0.60)
  waiting for transfers between devices: 517 us -> 143 us
  matrix products: 331 us -> 0 us
  Pallas kernels: 0 us -> 179 us
  starting transfers between devices: 0.21 us -> 158 us
  other arithmetic: 14.5 us -> 39 us
  between operations: 13.9 us -> 0.73 us
    psum x2 -> x0, waiting for transfers between devices: 343 us -> none  [from_root(): return lax.psum(block, axis)]
    dot_general x12 -> x0, matrix products: 331 us -> none  [the longest x6 166 us: body(): jnp.dot(green * screened[t], columns, precision=lax.Precision.HIGHEST, pr...]
    pallas_call x0 -> x8, Pallas kernels: none -> 179 us  [apply_chunk(): pl.pallas_call(functools.partial(apply_kernel, first), grid_spec=pltpu.Pr...]
    ppermute x0 -> x60, starting transfers between devices: none -> 158 us  [the longest x48 81.7 us: spread(): moving = lax.ppermute(moving, ('row', 'col'), pairs)]
    ppermute x0 -> x60, waiting for transfers between devices: none -> 143 us  [the longest x12 78.5 us: swap(): return lax.ppermute(value, 'col', [(i, i ^ bit) for i in range(n_col)])]
    reduce_scatter x2 -> x0, waiting for transfers between devices: 93.9 us -> none  [scatter_rows(): lax.psum_scatter(partial_value, 'col', scatter_dimension=0, tiled=True)]
    all_gather x2 -> x0, waiting for transfers between devices: 79.4 us -> none  [gather_rows(): return lax.all_gather(shard, 'col', axis=0, tiled=True)]
    add x0 -> x10, other arithmetic: none -> 33.4 us  [the longest x8 33.1 us: spread(): total = total + moving]
  transfers between devices with their start and end apart: 6 -> 60, of which waited for: 6 -> 13; matrix products, arithmetic and copies ran while one was open for 0% -> 6% of each run, Pallas kernels for 0% -> 13%
where the time goes in v1:
time: 534 us; the launch traced here: 527 us
  Pallas kernels  179 us (34%)
  starting transfers between devices  158 us (30%)
  waiting for transfers between devices  143 us (27%)
  other arithmetic  39 us (7%)
  local copies, waits for them, and re-layouts  6.49 us (1%)
    pallas_call x8, Pallas kernels, apply_chunk(): pl.pallas_call(functools.partial(apply_kernel, first), grid_spec=pltpu.Pr...  179 us
    ppermute x48, starting transfers between devices, spread(): moving = lax.ppermute(moving, ('row', 'col'), pairs)  81.7 us
    ppermute x12, waiting for transfers between devices, swap(): return lax.ppermute(value, 'col', [(i, i ^ bit) for i in range(n_col)])  78.5 us
    ppermute x12, starting transfers between devices, swap(): return lax.ppermute(value, 'col', [(i, i ^ bit) for i in range(n_col)])  76.6 us
    ppermute x48, waiting for transfers between devices, spread(): moving = lax.ppermute(moving, ('row', 'col'), pairs)  64.9 us
    add x8, other arithmetic, spread(): total = total + moving  33.1 us
  transfers between devices with their start and end apart: 60, of which 13 were waited for; matrix products, arithmetic and copies ran while one was open for 6% of the time, Pallas kernels for 13%

profile of v1, /device:TPU:0, one launch (start us, length us, event | category | flops | bytes accessed | tf_op | source)
XLA Modules:
  0.0 527.2 jit_solution(6676546899005838901)
XLA Ops:
  0.0 5.0 collective-permute-start.21
  5.9 13.0 %collective-permute-done.21 = f32[384,768]{1,0:T(8,128)S(1)} collective-permute-done((f32[384,768]{1,0:T(8,128)}, f32[384,768]{1,0:T(8,128)S(1)}, u32[]{:S(2)}, u32[]{:S(2)}) %collective-permute-start.21) | collective-permute-done | bytes 1179680 | tf_op jit(solution)/shard_map/ppermute | solution.py:132
  20.5 5.0 collective-permute-start.15
  26.2 8.2 %collective-permute-done.1 = f32[384,768]{1,0:T(8,128)S(1)} collective-permute-done((f32[384,768]{1,0:T(8,128)}, f32[384,768]{1,0:T(8,128)S(1)}, u32[]{:S(2)}, u32[]{:S(2)}) %collective-permute-start.1) | collective-permute-done | bytes 1179680 | tf_op jit(solution)/shard_map/ppermute | solution.py:96
  34.4 3.3 collective-permute-start.9
  37.7 1.7 collective-permute-start.12
  41.0 10.7 %collective-permute-done.9 = f32[384,768]{1,0:T(8,128)S(1)} collective-permute-done((f32[384,768]{1,0:T(8,128)S(1)}, f32[384,768]{1,0:T(8,128)S(1)}, u32[]{:S(2)}, u32[]{:S(2)}) %collective-permute-start.9) | collective-permute-done | bytes 1179680 | tf_op jit(solution)/shard_map/ppermute | solution.py:132
  51.7 1.7 collective-permute-start.16
  53.4 1.7 collective-permute-start.19
  55.1 6.1 %collective-permute-start.3 = (f32[384,768]{1,0:T(8,128)S(1)}, f32[384,768]{1,0:T(8,128)}, u32[]{:S(2)}, u32[]{:S(2)}) collective-permute-start(f32[384,768]{1,0:T(8,128)S(1)} %collective-permute-done.2), channel_id=1, source_target_pairs={{0,4},{5,9},{10,14},{16,20},{21,25},{26,30}} | collective-permute-start | bytes 3538952 | tf_op jit(solution)/shard_map/ppermute | solution.py:132
  61.2 1.8 collective-permute-start.6
  63.7 1.7 collective-permute-start.13
  65.4 1.7 collective-permute-start.17
  67.0 6.8 %collective-permute-done.3 = f32[384,768]{1,0:T(8,128)} collective-permute-done((f32[384,768]{1,0:T(8,128)S(1)}, f32[384,768]{1,0:T(8,128)}, u32[]{:S(2)}, u32[]{:S(2)}) %collective-permute-start.3) | collective-permute-done | bytes 1179680 | tf_op jit(solution)/shard_map/ppermute | solution.py:132
  73.8 1.7 collective-permute-start.4
  75.5 1.7 collective-permute-start.7
  77.2 1.7 collective-permute-start.20
  86.0 5.1 add_add_fusion.4
  91.1 4.4 add_add_fusion.5
  95.5 3.7 add_add_fusion.6
  99.2 4.3 add_add_fusion.7
  103.5 22.2 %apply_chunk.8.rest_0_ = f32[1536,768]{1,0:T(8,128)} custom-call(s32[5]{0:T(128)} %stack.23.place, f32[1536,768]{1,0:T(8,128)} %get-tuple-element.16.rows_ref, f32[384,768]{1,0:T(8,128)} %get-tuple-element.9.cols_ref, f32[3,768]{1,0:T(4,128)} %broadcast_multiply_fusion.weight_ref, f32[3,1536,1536]{2,1,0:T(8,128)} %screened_ref.15), custom_call_target="tpu_custom_call" | custom-call | flops 10871635968 | bytes 21233664 | tf_op jit(solution)/shard_map/apply_chunk/pallas_call | solution.py:69
  125.7 22.4 %apply_chunk.9.rest_0_ = f32[1536,768]{1,0:T(8,128)} custom-call(s32[5]{0:T(128)} %stack.22.place, f32[1536,768]{1,0:T(8,128)} %get-tuple-element.16.rows_ref, f32[384,768]{1,0:T(8,128)} %get-tuple-element.11.cols_ref, f32[3,768]{1,0:T(4,128)} %broadcast_multiply_fusion.weight_ref, f32[3,1536,1536]{2,1,0:T(8,128)} %screened_ref.15, ...), custom_call_target="tpu_custom_call", output_to_operand_aliasing={{}: (5, {})} | custom-call | flops 10871635968 | bytes 21233664 | tf_op jit(solution)/shard_map/apply_chunk/pallas_call | solution.py:69
  148.1 22.4 %apply_chunk.10.rest_0_ = f32[1536,768]{1,0:T(8,128)} custom-call(s32[5]{0:T(128)} %stack.21.place, f32[1536,768]{1,0:T(8,128)} %get-tuple-element.16.rows_ref, f32[384,768]{1,0:T(8,128)} %get-tuple-element.13.cols_ref, f32[3,768]{1,0:T(4,128)} %broadcast_multiply_fusion.weight_ref, f32[3,1536,1536]{2,1,0:T(8,128)} %screened_ref.15, ...), custom_call_target="tpu_custom_call", output_to_operand_aliasing={{}: (5, {})} | custom-call | flops 10871635968 | bytes 21233664 | tf_op jit(solution)/shard_map/apply_chunk/pallas_call | solution.py:69
  170.5 22.6 %apply_chunk.11 = f32[1536,768]{1,0:T(8,128)} custom-call(s32[5]{0:T(128)} %stack.20.place, f32[1536,768]{1,0:T(8,128)} %get-tuple-element.16.rows_ref, f32[384,768]{1,0:T(8,128)} %get-tuple-element.15.cols_ref, f32[3,768]{1,0:T(4,128)} %broadcast_multiply_fusion.weight_ref, f32[3,1536,1536]{2,1,0:T(8,128)} %screened_ref.15, ...), custom_call_target="tpu_custom_call", output_to_operand_aliasing={{}: (5, {})} | custom-call | flops 10871635968 | bytes 21233664 | tf_op jit(solution)/shard_map/apply_chunk/pallas_call | solution.py:69
  193.0 1.9 fusion.5
  195.0 15.2 %collective-permute-start.28 = (f32[384,768]{1,0:T(8,128)S(1)}, f32[384,768]{1,0:T(8,128)S(1)}, u32[]{:S(2)}, u32[]{:S(2)}) collective-permute-start(f32[384,768]{1,0:T(8,128)S(1)} %get-tuple-element.8), channel_id=1, source_target_pairs={{0,1},{1,0},{2,3},{3,2},{4,5},{5,4},{6,7},{7,6},{8,9},{9,8},{10,11... | collective-permute-start | bytes 3538952 | tf_op jit(solution)/shard_map/ppermute | solution.py:96
  210.3 2.4 collective-permute-done.28
  212.8 35.9 %collective-permute-start.29 = (f32[384,768]{1,0:T(8,128)S(1)}, f32[384,768]{1,0:T(8,128)S(1)}, u32[]{:S(2)}, u32[]{:S(2)}) collective-permute-start(f32[384,768]{1,0:T(8,128)S(1)} %slice_add_fusion.2), channel_id=1, source_target_pairs={{0,2},{1,3},{2,0},{3,1},{4,6},{5,7},{6,4},{7,5},{8,10},{9,11},{10,... | collective-permute-start | bytes 3538952 | tf_op jit(solution)/shard_map/ppermute | solution.py:96
  248.8 26.3 %collective-permute-done.29 = f32[384,768]{1,0:T(8,128)S(1)} collective-permute-done((f32[384,768]{1,0:T(8,128)S(1)}, f32[384,768]{1,0:T(8,128)S(1)}, u32[]{:S(2)}, u32[]{:S(2)}) %collective-permute-start.29) | collective-permute-done | bytes 1179680 | tf_op jit(solution)/shard_map/ppermute | solution.py:96
  278.6 11.9 %collective-permute-done.51 = f32[384,768]{1,0:T(8,128)S(1)} collective-permute-done((f32[384,768]{1,0:T(8,128)S(1)}, f32[384,768]{1,0:T(8,128)S(1)}, u32[]{:S(2)}, u32[]{:S(2)}) %collective-permute-start.51) | collective-permute-done | bytes 1179680 | tf_op jit(solution)/shard_map/ppermute | solution.py:132
  292.0 12.9 %collective-permute-done.31 = f32[384,768]{1,0:T(8,128)S(1)} collective-permute-done((f32[384,768]{1,0:T(8,128)S(1)}, f32[384,768]{1,0:T(8,128)S(1)}, u32[]{:S(2)}, u32[]{:S(2)}) %collective-permute-start.31) | collective-permute-done | bytes 1179680 | tf_op jit(solution)/shard_map/ppermute | solution.py:96
  305.0 2.7 collective-permute-start.45
  310.0 1.7 collective-permute-start.42
  312.4 8.9 %collective-permute-done.45 = f32[384,768]{1,0:T(8,128)S(1)} collective-permute-done((f32[384,768]{1,0:T(8,128)S(1)}, f32[384,768]{1,0:T(8,128)S(1)}, u32[]{:S(2)}, u32[]{:S(2)}) %collective-permute-start.45) | collective-permute-done | bytes 1179680 | tf_op jit(solution)/shard_map/ppermute | solution.py:132
  322.0 1.7 collective-permute-start.46
  323.7 10.2 %collective-permute-done.39 = f32[384,768]{1,0:T(8,128)S(1)} collective-permute-done((f32[384,768]{1,0:T(8,128)S(1)}, f32[384,768]{1,0:T(8,128)S(1)}, u32[]{:S(2)}, u32[]{:S(2)}) %collective-permute-start.39) | collective-permute-done | bytes 1179680 | tf_op jit(solution)/shard_map/ppermute | solution.py:132
  333.9 1.7 collective-permute-start.49
  336.3 6.1 %collective-permute-start.33 = (f32[384,768]{1,0:T(8,128)S(1)}, f32[384,768]{1,0:T(8,128)}, u32[]{:S(2)}, u32[]{:S(2)}) collective-permute-start(f32[384,768]{1,0:T(8,128)S(1)} %collective-permute-done.32), channel_id=1, source_target_pairs={{0,4},{5,9},{10,14},{16,20},{21,25},{26,30}} | collective-permute-start | bytes 3538952 | tf_op jit(solution)/shard_map/ppermute | solution.py:132
  342.4 1.7 collective-permute-start.36
  344.1 2.5 pad_maximum_fusion.rows_ref
  346.6 1.7 collective-permute-start.43
  348.3 1.7 collective-permute-start.47
  350.0 1.7 collective-permute-start.50
  351.7 3.3 collective-permute-done.33
  355.0 1.7 collective-permute-start.34
  356.8 1.7 collective-permute-start.37
  358.4 1.6 add_add_fusion.cols_ref
  360.0 22.4 %apply_chunk.12.rest_0_ = f32[1536,768]{1,0:T(8,128)} custom-call(s32[5]{0:T(128)} %stack.23.place, f32[1536,768]{1,0:T(8,128)} %pad_maximum_fusion.rows_ref, f32[384,768]{1,0:T(8,128)} %add_add_fusion.cols_ref, f32[3,768]{1,0:T(4,128)} %broadcast_multiply_fusion.weight_ref, f32[3,1536,1536]{2,1,0:T(8,128)} %screened_ref.15), custom_call_target="tpu_custom_call" | custom-call | flops 10871635968 | bytes 21233664 | tf_op jit(solution)/shard_map/apply_chunk/pallas_call | solution.py:69
  382.4 1.7 collective-permute-start.41
  384.1 1.7 collective-permute-start.44
  385.8 1.7 collective-permute-start.35
  387.5 1.7 collective-permute-start.38
  389.2 4.9 add_add_fusion.1.cols_ref
  394.1 22.4 %apply_chunk.13.rest_0_ = f32[1536,768]{1,0:T(8,128)} custom-call(s32[5]{0:T(128)} %stack.22.place, f32[1536,768]{1,0:T(8,128)} %pad_maximum_fusion.rows_ref, f32[384,768]{1,0:T(8,128)} %add_add_fusion.1.cols_ref, f32[3,768]{1,0:T(4,128)} %broadcast_multiply_fusion.weight_ref, f32[3,1536,1536]{2,1,0:T(8,128)} %screened_ref.15, ...), custom_call_target="tpu_custom_call", output_to_operand_aliasing={{}: (5, {})} | custom-call | flops 10871635968 | bytes 21233664 | tf_op jit(solution)/shard_map/apply_chunk/pallas_call | solution.py:69
  416.5 4.6 add_add_fusion.2.cols_ref
  421.1 22.4 %apply_chunk.14.rest_0_ = f32[1536,768]{1,0:T(8,128)} custom-call(s32[5]{0:T(128)} %stack.21.place, f32[1536,768]{1,0:T(8,128)} %pad_maximum_fusion.rows_ref, f32[384,768]{1,0:T(8,128)} %add_add_fusion.2.cols_ref, f32[3,768]{1,0:T(4,128)} %broadcast_multiply_fusion.weight_ref, f32[3,1536,1536]{2,1,0:T(8,128)} %screened_ref.15, ...), custom_call_target="tpu_custom_call", output_to_operand_aliasing={{}: (5, {})} | custom-call | flops 10871635968 | bytes 21233664 | tf_op jit(solution)/shard_map/apply_chunk/pallas_call | solution.py:69
  443.5 4.6 add_add_fusion.3.cols_ref
  448.1 22.6 %apply_chunk.15 = f32[1536,768]{1,0:T(8,128)} custom-call(s32[5]{0:T(128)} %stack.20.place, f32[1536,768]{1,0:T(8,128)} %pad_maximum_fusion.rows_ref, f32[384,768]{1,0:T(8,128)} %add_add_fusion.3.cols_ref, f32[3,768]{1,0:T(4,128)} %broadcast_multiply_fusion.weight_ref, f32[3,1536,1536]{2,1,0:T(8,128)} %screened_ref.15, ...), custom_call_target="tpu_custom_call", output_to_operand_aliasing={{}: (5, {})} | custom-call | flops 10871635968 | bytes 21233664 | tf_op jit(solution)/shard_map/apply_chunk/pallas_call | solution.py:69
  470.6 1.9 fusion.4
  472.6 8.4 %collective-permute-start.58 = (f32[384,768]{1,0:T(8,128)S(1)}, f32[384,768]{1,0:T(8,128)S(1)}, u32[]{:S(2)}, u32[]{:S(2)}) collective-permute-start(f32[384,768]{1,0:T(8,128)S(1)} %get-tuple-element.6), channel_id=1, source_target_pairs={{0,1},{1,0},{2,3},{3,2},{4,5},{5,4},{6,7},{7,6},{8,9},{9,8},{10,11... | collective-permute-start | bytes 3538952 | tf_op jit(solution)/shard_map/ppermute | solution.py:96
  481.0 2.4 collective-permute-done.58
  483.6 15.7 %collective-permute-start.59 = (f32[384,768]{1,0:T(8,128)S(1)}, f32[384,768]{1,0:T(8,128)S(1)}, u32[]{:S(2)}, u32[]{:S(2)}) collective-permute-start(f32[384,768]{1,0:T(8,128)S(1)} %slice_add_fusion), channel_id=1, source_target_pairs={{0,2},{1,3},{2,0},{3,1},{4,6},{5,7},{6,4},{7,5},{8,10},{9,11},{10,... | collective-permute-start | bytes 3538952 | tf_op jit(solution)/shard_map/ppermute | solution.py:96
  499.3 26.3 %collective-permute-done.59 = f32[384,768]{1,0:T(8,128)S(1)} collective-permute-done((f32[384,768]{1,0:T(8,128)S(1)}, f32[384,768]{1,0:T(8,128)S(1)}, u32[]{:S(2)}, u32[]{:S(2)}) %collective-permute-start.59) | collective-permute-done | bytes 1179680 | tf_op jit(solution)/shard_map/ppermute | solution.py:96
  (130 shorter events, 23.9 us)
Async XLA Ops:
  0.0 18.9 %collective-permute-start.21 = (f32[384,768]{1,0:T(8,128)}, f32[384,768]{1,0:T(8,128)S(1)}, u32[]{:S(2)}, u32[]{:S(2)}) collective-permute-start(f32[384,768]{1,0:T(8,128)} %param.4), channel_id=1, source_target_pairs={{0,4},{5,9},{10,14},{16,20},{21,25},{26,30}} | collective-permute-start | bytes 3538952 | tf_op jit(solution)/shard_map/ppermute | solution.py:132
  5.0 14.7 %collective-permute-start.24 = (f32[384,768]{1,0:T(8,128)}, f32[384,768]{1,0:T(8,128)S(1)}, u32[]{:S(2)}, u32[]{:S(2)}) collective-permute-start(f32[384,768]{1,0:T(8,128)} %param.4), channel_id=1, source_target_pairs={{5,1},{10,6},{15,11},{21,17},{26,22},{31,27}} | collective-permute-start | bytes 3538952 | tf_op jit(solution)/shard_map/ppermute | solution.py:132
  5.7 14.7 %collective-permute-start = (f32[384,768]{1,0:T(8,128)}, f32[384,768]{1,0:T(8,128)S(1)}, u32[]{:S(2)}, u32[]{:S(2)}) collective-permute-start(f32[384,768]{1,0:T(8,128)} %param.4), channel_id=1, source_target_pairs={{0,1},{1,0},{2,3},{3,2},{4,5},{5,4},{6,7},{7,6},{8,9},{9,8},{10,11... | collective-permute-start | bytes 3538952 | tf_op jit(solution)/shard_map/ppermute | solution.py:96
  5.8 28.6 %collective-permute-start.1 = (f32[384,768]{1,0:T(8,128)}, f32[384,768]{1,0:T(8,128)S(1)}, u32[]{:S(2)}, u32[]{:S(2)}) collective-permute-start(f32[384,768]{1,0:T(8,128)} %param.4), channel_id=1, source_target_pairs={{0,2},{1,3},{2,0},{3,1},{4,6},{5,7},{6,4},{7,5},{8,10},{9,11},{10,... | collective-permute-start | bytes 3538952 | tf_op jit(solution)/shard_map/ppermute | solution.py:96
  18.9 18.8 %collective-permute-start.22 = (f32[384,768]{1,0:T(8,128)S(1)}, f32[384,768]{1,0:T(8,128)S(1)}, u32[]{:S(2)}, u32[]{:S(2)}) collective-permute-start(f32[384,768]{1,0:T(8,128)S(1)} %collective-permute-done.21), channel_id=1, source_target_pairs={{4,8},{9,13},{20,24},{25,29}} | collective-permute-start | bytes 3538952 | tf_op jit(solution)/shard_map/ppermute | solution.py:132
  19.7 19.8 %collective-permute-start.25 = (f32[384,768]{1,0:T(8,128)S(1)}, f32[384,768]{1,0:T(8,128)S(1)}, u32[]{:S(2)}, u32[]{:S(2)}) collective-permute-start(f32[384,768]{1,0:T(8,128)S(1)} %collective-permute-done.24), channel_id=1, source_target_pairs={{6,2},{11,7},{22,18},{27,23}} | collective-permute-start | bytes 3538952 | tf_op jit(solution)/shard_map/ppermute | solution.py:132
  20.5 19.0 %collective-permute-start.15 = (f32[384,768]{1,0:T(8,128)S(1)}, f32[384,768]{1,0:T(8,128)S(1)}, u32[]{:S(2)}, u32[]{:S(2)}) collective-permute-start(f32[384,768]{1,0:T(8,128)S(1)} %collective-permute-done), channel_id=1, source_target_pairs={{0,4},{5,9},{10,14},{16,20},{21,25},{26,30}} | collective-permute-start | bytes 3538952 | tf_op jit(solution)/shard_map/ppermute | solution.py:132
  25.4 14.8 %collective-permute-start.18 = (f32[384,768]{1,0:T(8,128)S(1)}, f32[384,768]{1,0:T(8,128)S(1)}, u32[]{:S(2)}, u32[]{:S(2)}) collective-permute-start(f32[384,768]{1,0:T(8,128)S(1)} %collective-permute-done), channel_id=1, source_target_pairs={{5,1},{10,6},{15,11},{21,17},{26,22},{31,27}} | collective-permute-start | bytes 3538952 | tf_op jit(solution)/shard_map/ppermute | solution.py:132
  34.4 17.3 %collective-permute-start.9 = (f32[384,768]{1,0:T(8,128)S(1)}, f32[384,768]{1,0:T(8,128)S(1)}, u32[]{:S(2)}, u32[]{:S(2)}) collective-permute-start(f32[384,768]{1,0:T(8,128)S(1)} %collective-permute-done.1), channel_id=1, source_target_pairs={{0,4},{5,9},{10,14},{16,20},{21,25},{26,30}} | collective-permute-start | bytes 3538952 | tf_op jit(solution)/shard_map/ppermute | solution.py:132
  37.7 39.5 %copy-start.13 = (f32[384,768]{1,0:T(8,128)}, f32[384,768]{1,0:T(8,128)S(1)}, u32[]{:S(2)}) copy-start(f32[384,768]{1,0:T(8,128)S(1)} %collective-permute-done.22) | copy-start | bytes 3538948
  37.7 15.7 %collective-permute-start.12 = (f32[384,768]{1,0:T(8,128)S(1)}, f32[384,768]{1,0:T(8,128)}, u32[]{:S(2)}, u32[]{:S(2)}) collective-permute-start(f32[384,768]{1,0:T(8,128)S(1)} %collective-permute-done.1), channel_id=1, source_target_pairs={{5,1},{10,6},{15,11},{21,17},{26,22},{31,27}} | collective-permute-start | bytes 3538952 | tf_op jit(solution)/shard_map/ppermute | solution.py:132
  39.5 39.4 %copy-start.16 = (f32[384,768]{1,0:T(8,128)}, f32[384,768]{1,0:T(8,128)S(1)}, u32[]{:S(2)}) copy-start(f32[384,768]{1,0:T(8,128)S(1)} %collective-permute-done.25) | copy-start | bytes 3538948
  39.5 15.6 %collective-permute-start.2 = (f32[384,768]{1,0:T(8,128)S(1)}, f32[384,768]{1,0:T(8,128)S(1)}, u32[]{:S(2)}, u32[]{:S(2)}) collective-permute-start(f32[384,768]{1,0:T(8,128)S(1)} %collective-permute-done.1), channel_id=1, source_target_pairs={{0,1},{1,0},{2,3},{3,2},{4,5},{5,4},{6,7},{7,6},{8,9},{9,8},{10,11... | collective-permute-start | bytes 3538952 | tf_op jit(solution)/shard_map/ppermute | solution.py:96
  39.5 21.7 %collective-permute-start.23 = (f32[384,768]{1,0:T(8,128)S(1)}, f32[384,768]{1,0:T(8,128)S(1)}, u32[]{:S(2)}, u32[]{:S(2)}) collective-permute-start(f32[384,768]{1,0:T(8,128)S(1)} %collective-permute-done.22), channel_id=1, source_target_pairs={{8,12},{24,28}} | collective-permute-start | bytes 3538952 | tf_op jit(solution)/shard_map/ppermute | solution.py:132
  40.2 22.7 %collective-permute-start.26 = (f32[384,768]{1,0:T(8,128)S(1)}, f32[384,768]{1,0:T(8,128)S(1)}, u32[]{:S(2)}, u32[]{:S(2)}) collective-permute-start(f32[384,768]{1,0:T(8,128)S(1)} %collective-permute-done.25), channel_id=1, source_target_pairs={{7,3},{23,19}} | collective-permute-start | bytes 3538952 | tf_op jit(solution)/shard_map/ppermute | solution.py:132
  51.7 11.9 %collective-permute-start.16 = (f32[384,768]{1,0:T(8,128)S(1)}, f32[384,768]{1,0:T(8,128)}, u32[]{:S(2)}, u32[]{:S(2)}) collective-permute-start(f32[384,768]{1,0:T(8,128)S(1)} %collective-permute-done.15), channel_id=1, source_target_pairs={{4,8},{9,13},{20,24},{25,29}} | collective-permute-start | bytes 3538952 | tf_op jit(solution)/shard_map/ppermute | solution.py:132
  53.4 11.9 %collective-permute-start.19 = (f32[384,768]{1,0:T(8,128)S(1)}, f32[384,768]{1,0:T(8,128)}, u32[]{:S(2)}, u32[]{:S(2)}) collective-permute-start(f32[384,768]{1,0:T(8,128)S(1)} %collective-permute-done.18), channel_id=1, source_target_pairs={{6,2},{11,7},{22,18},{27,23}} | collective-permute-start | bytes 3538952 | tf_op jit(solution)/shard_map/ppermute | solution.py:132
  55.1 18.7 %collective-permute-start.3 = (f32[384,768]{1,0:T(8,128)S(1)}, f32[384,768]{1,0:T(8,128)}, u32[]{:S(2)}, u32[]{:S(2)}) collective-permute-start(f32[384,768]{1,0:T(8,128)S(1)} %collective-permute-done.2), channel_id=1, source_target_pairs={{0,4},{5,9},{10,14},{16,20},{21,25},{26,30}} | collective-permute-start | bytes 3538952 | tf_op jit(solution)/shard_map/ppermute | solution.py:132
  61.2 14.3 %collective-permute-start.6 = (f32[384,768]{1,0:T(8,128)S(1)}, f32[384,768]{1,0:T(8,128)}, u32[]{:S(2)}, u32[]{:S(2)}) collective-permute-start(f32[384,768]{1,0:T(8,128)S(1)} %collective-permute-done.2), channel_id=1, source_target_pairs={{5,1},{10,6},{15,11},{21,17},{26,22},{31,27}} | collective-permute-start | bytes 3538952 | tf_op jit(solution)/shard_map/ppermute | solution.py:132
  62.9 14.3 %collective-permute-start.10 = (f32[384,768]{1,0:T(8,128)S(1)}, f32[384,768]{1,0:T(8,128)S(1)}, u32[]{:S(2)}, u32[]{:S(2)}) collective-permute-start(f32[384,768]{1,0:T(8,128)S(1)} %collective-permute-done.9), channel_id=1, source_target_pairs={{4,8},{9,13},{20,24},{25,29}} | collective-permute-start | bytes 3538952 | tf_op jit(solution)/shard_map/ppermute | solution.py:132
  63.7 17.8 %collective-permute-start.13 = (f32[384,768]{1,0:T(8,128)}, f32[384,768]{1,0:T(8,128)}, u32[]{:S(2)}, u32[]{:S(2)}) collective-permute-start(f32[384,768]{1,0:T(8,128)} %collective-permute-done.12), channel_id=1, source_target_pairs={{6,2},{11,7},{22,18},{27,23}} | collective-permute-start | bytes 3538952 | tf_op jit(solution)/shard_map/ppermute | solution.py:132
  65.4 16.8 %collective-permute-start.17 = (f32[384,768]{1,0:T(8,128)}, f32[384,768]{1,0:T(8,128)}, u32[]{:S(2)}, u32[]{:S(2)}) collective-permute-start(f32[384,768]{1,0:T(8,128)} %collective-permute-done.16), channel_id=1, source_target_pairs={{8,12},{24,28}} | collective-permute-start | bytes 3538952 | tf_op jit(solution)/shard_map/ppermute | solution.py:132
  73.8 10.5 %collective-permute-start.4 = (f32[384,768]{1,0:T(8,128)}, f32[384,768]{1,0:T(8,128)}, u32[]{:S(2)}, u32[]{:S(2)}) collective-permute-start(f32[384,768]{1,0:T(8,128)} %collective-permute-done.3), channel_id=1, source_target_pairs={{4,8},{9,13},{20,24},{25,29}} | collective-permute-start | bytes 3538952 | tf_op jit(solution)/shard_map/ppermute | solution.py:132
  75.5 9.7 %collective-permute-start.7 = (f32[384,768]{1,0:T(8,128)}, f32[384,768]{1,0:T(8,128)}, u32[]{:S(2)}, u32[]{:S(2)}) collective-permute-start(f32[384,768]{1,0:T(8,128)} %collective-permute-done.6), channel_id=1, source_target_pairs={{6,2},{11,7},{22,18},{27,23}} | collective-permute-start | bytes 3538952 | tf_op jit(solution)/shard_map/ppermute | solution.py:132
  77.2 13.8 %collective-permute-start.20 = (f32[384,768]{1,0:T(8,128)}, f32[384,768]{1,0:T(8,128)}, u32[]{:S(2)}, u32[]{:S(2)}) collective-permute-start(f32[384,768]{1,0:T(8,128)} %collective-permute-done.19), channel_id=1, source_target_pairs={{7,3},{23,19}} | collective-permute-start | bytes 3538952 | tf_op jit(solution)/shard_map/ppermute | solution.py:132
  81.5 14.0 %collective-permute-start.11 = (f32[384,768]{1,0:T(8,128)}, f32[384,768]{1,0:T(8,128)S(1)}, u32[]{:S(2)}, u32[]{:S(2)}) collective-permute-start(f32[384,768]{1,0:T(8,128)} %copy-done.21), channel_id=1, source_target_pairs={{8,12},{24,28}} | collective-permute-start | bytes 3538952 | tf_op jit(solution)/shard_map/ppermute | solution.py:132
  82.2 13.3 %collective-permute-start.14 = (f32[384,768]{1,0:T(8,128)}, f32[384,768]{1,0:T(8,128)S(1)}, u32[]{:S(2)}, u32[]{:S(2)}) collective-permute-start(f32[384,768]{1,0:T(8,128)} %collective-permute-done.13), channel_id=1, source_target_pairs={{7,3},{23,19}} | collective-permute-start | bytes 3538952 | tf_op jit(solution)/shard_map/ppermute | solution.py:132
  84.3 14.9 %collective-permute-start.5 = (f32[384,768]{1,0:T(8,128)}, f32[384,768]{1,0:T(8,128)S(1)}, u32[]{:S(2)}, u32[]{:S(2)}) collective-permute-start(f32[384,768]{1,0:T(8,128)} %collective-permute-done.4), channel_id=1, source_target_pairs={{8,12},{24,28}} | collective-permute-start | bytes 3538952 | tf_op jit(solution)/shard_map/ppermute | solution.py:132
  85.2 14.0 %collective-permute-start.8 = (f32[384,768]{1,0:T(8,128)}, f32[384,768]{1,0:T(8,128)S(1)}, u32[]{:S(2)}, u32[]{:S(2)}) collective-permute-start(f32[384,768]{1,0:T(8,128)} %collective-permute-done.7), channel_id=1, source_target_pairs={{7,3},{23,19}} | collective-permute-start | bytes 3538952 | tf_op jit(solution)/shard_map/ppermute | solution.py:132
  195.0 17.7 %collective-permute-start.28 = (f32[384,768]{1,0:T(8,128)S(1)}, f32[384,768]{1,0:T(8,128)S(1)}, u32[]{:S(2)}, u32[]{:S(2)}) collective-permute-start(f32[384,768]{1,0:T(8,128)S(1)} %get-tuple-element.8), channel_id=1, source_target_pairs={{0,1},{1,0},{2,3},{3,2},{4,5},{5,4},{6,7},{7,6},{8,9},{9,8},{10,11... | collective-permute-start | bytes 3538952 | tf_op jit(solution)/shard_map/ppermute | solution.py:96
  210.2 64.8 %copy-start.3 = (f32[384,768]{1,0:T(8,128)S(1)}, f32[384,768]{1,0:T(8,128)}, u32[]{:S(2)}) copy-start(f32[384,768]{1,0:T(8,128)} %param.4) | copy-start | bytes 3538948
  210.2 38.6 %collective-permute-start.27 = (f32[384,768]{1,0:T(8,128)S(1)}, f32[384,768]{1,0:T(8,128)S(1)}, u32[]{:S(2)}, u32[]{:S(2)}) collective-permute-start(f32[384,768]{1,0:T(8,128)S(1)} %get-tuple-element.7), channel_id=1, source_target_pairs={{0,1},{1,0},{2,3},{3,2},{4,5},{5,4},{6,7},{7,6},{8,9},{9,8},{10,11... | collective-permute-start | bytes 3538952 | tf_op jit(solution)/shard_map/ppermute | solution.py:96
  212.8 62.2 %collective-permute-start.29 = (f32[384,768]{1,0:T(8,128)S(1)}, f32[384,768]{1,0:T(8,128)S(1)}, u32[]{:S(2)}, u32[]{:S(2)}) collective-permute-start(f32[384,768]{1,0:T(8,128)S(1)} %slice_add_fusion.2), channel_id=1, source_target_pairs={{0,2},{1,3},{2,0},{3,1},{4,6},{5,7},{6,4},{7,5},{8,10},{9,11},{10,... | collective-permute-start | bytes 3538952 | tf_op jit(solution)/shard_map/ppermute | solution.py:96
  275.3 15.2 %collective-permute-start.51 = (f32[384,768]{1,0:T(8,128)S(1)}, f32[384,768]{1,0:T(8,128)S(1)}, u32[]{:S(2)}, u32[]{:S(2)}) collective-permute-start(f32[384,768]{1,0:T(8,128)S(1)} %fusion.3), channel_id=1, source_target_pairs={{0,4},{5,9},{10,14},{16,20},{21,25},{26,30}} | collective-permute-start | bytes 3538952 | tf_op jit(solution)/shard_map/ppermute | solution.py:132
  276.9 14.4 %collective-permute-start.54 = (f32[384,768]{1,0:T(8,128)S(1)}, f32[384,768]{1,0:T(8,128)S(1)}, u32[]{:S(2)}, u32[]{:S(2)}) collective-permute-start(f32[384,768]{1,0:T(8,128)S(1)} %fusion.3), channel_id=1, source_target_pairs={{5,1},{10,6},{15,11},{21,17},{26,22},{31,27}} | collective-permute-start | bytes 3538952 | tf_op jit(solution)/shard_map/ppermute | solution.py:132
  277.6 27.3 %collective-permute-start.31 = (f32[384,768]{1,0:T(8,128)S(1)}, f32[384,768]{1,0:T(8,128)S(1)}, u32[]{:S(2)}, u32[]{:S(2)}) collective-permute-start(f32[384,768]{1,0:T(8,128)S(1)} %fusion.3), channel_id=1, source_target_pairs={{0,2},{1,3},{2,0},{3,1},{4,6},{5,7},{6,4},{7,5},{8,10},{9,11},{10,... | collective-permute-start | bytes 3538952 | tf_op jit(solution)/shard_map/ppermute | solution.py:96
  278.6 26.3 %collective-permute-start.30 = (f32[384,768]{1,0:T(8,128)S(1)}, f32[384,768]{1,0:T(8,128)S(1)}, u32[]{:S(2)}, u32[]{:S(2)}) collective-permute-start(f32[384,768]{1,0:T(8,128)S(1)} %fusion.3), channel_id=1, source_target_pairs={{0,1},{1,0},{2,3},{3,2},{4,5},{5,4},{6,7},{7,6},{8,9},{9,8},{10,11... | collective-permute-start | bytes 3538952 | tf_op jit(solution)/shard_map/ppermute | solution.py:96
  290.5 17.9 %collective-permute-start.52 = (f32[384,768]{1,0:T(8,128)S(1)}, f32[384,768]{1,0:T(8,128)S(1)}, u32[]{:S(2)}, u32[]{:S(2)}) collective-permute-start(f32[384,768]{1,0:T(8,128)S(1)} %collective-permute-done.51), channel_id=1, source_target_pairs={{4,8},{9,13},{20,24},{25,29}} | collective-permute-start | bytes 3538952 | tf_op jit(solution)/shard_map/ppermute | solution.py:132
  291.2 18.7 %collective-permute-start.55 = (f32[384,768]{1,0:T(8,128)S(1)}, f32[384,768]{1,0:T(8,128)S(1)}, u32[]{:S(2)}, u32[]{:S(2)}) collective-permute-start(f32[384,768]{1,0:T(8,128)S(1)} %collective-permute-done.54), channel_id=1, source_target_pairs={{6,2},{11,7},{22,18},{27,23}} | collective-permute-start | bytes 3538952 | tf_op jit(solution)/shard_map/ppermute | solution.py:132
  304.9 6.7 %collective-permute-start.32 = (f32[384,768]{1,0:T(8,128)S(1)}, f32[384,768]{1,0:T(8,128)S(1)}, u32[]{:S(2)}, u32[]{:S(2)}) collective-permute-start(f32[384,768]{1,0:T(8,128)S(1)} %collective-permute-done.31), channel_id=1, source_target_pairs={{0,1},{1,0},{2,3},{3,2},{4,5},{5,4},{6,7},{7,6},{8,9},{9,8},{10,11... | collective-permute-start | bytes 3538952 | tf_op jit(solution)/shard_map/ppermute | solution.py:96
  304.9 41.6 %copy-start.2 = (f32[384,768]{1,0:T(8,128)}, f32[384,768]{1,0:T(8,128)S(1)}, u32[]{:S(2)}) copy-start(f32[384,768]{1,0:T(8,128)S(1)} %collective-permute-done.30) | copy-start | bytes 3538948
  305.0 16.3 %collective-permute-start.45 = (f32[384,768]{1,0:T(8,128)S(1)}, f32[384,768]{1,0:T(8,128)S(1)}, u32[]{:S(2)}, u32[]{:S(2)}) collective-permute-start(f32[384,768]{1,0:T(8,128)S(1)} %collective-permute-done.30), channel_id=1, source_target_pairs={{0,4},{5,9},{10,14},{16,20},{21,25},{26,30}} | collective-permute-start | bytes 3538952 | tf_op jit(solution)/shard_map/ppermute | solution.py:132
  307.6 14.4 %collective-permute-start.48 = (f32[384,768]{1,0:T(8,128)S(1)}, f32[384,768]{1,0:T(8,128)S(1)}, u32[]{:S(2)}, u32[]{:S(2)}) collective-permute-start(f32[384,768]{1,0:T(8,128)S(1)} %collective-permute-done.30), channel_id=1, source_target_pairs={{5,1},{10,6},{15,11},{21,17},{26,22},{31,27}} | collective-permute-start | bytes 3538952 | tf_op jit(solution)/shard_map/ppermute | solution.py:132
  308.4 25.5 %collective-permute-start.39 = (f32[384,768]{1,0:T(8,128)S(1)}, f32[384,768]{1,0:T(8,128)S(1)}, u32[]{:S(2)}, u32[]{:S(2)}) collective-permute-start(f32[384,768]{1,0:T(8,128)S(1)} %collective-permute-done.31), channel_id=1, source_target_pairs={{0,4},{5,9},{10,14},{16,20},{21,25},{26,30}} | collective-permute-start | bytes 3538952 | tf_op jit(solution)/shard_map/ppermute | solution.py:132
  310.0 25.6 %collective-permute-start.42 = (f32[384,768]{1,0:T(8,128)S(1)}, f32[384,768]{1,0:T(8,128)}, u32[]{:S(2)}, u32[]{:S(2)}) collective-permute-start(f32[384,768]{1,0:T(8,128)S(1)} %collective-permute-done.31), channel_id=1, source_target_pairs={{5,1},{10,6},{15,11},{21,17},{26,22},{31,27}} | collective-permute-start | bytes 3538952 | tf_op jit(solution)/shard_map/ppermute | solution.py:132
  311.6 24.7 %collective-permute-start.53 = (f32[384,768]{1,0:T(8,128)S(1)}, f32[384,768]{1,0:T(8,128)S(1)}, u32[]{:S(2)}, u32[]{:S(2)}) collective-permute-start(f32[384,768]{1,0:T(8,128)S(1)} %collective-permute-done.52), channel_id=1, source_target_pairs={{8,12},{24,28}} | collective-permute-start | bytes 3538952 | tf_op jit(solution)/shard_map/ppermute | solution.py:132
  321.3 21.1 %collective-permute-start.56 = (f32[384,768]{1,0:T(8,128)S(1)}, f32[384,768]{1,0:T(8,128)S(1)}, u32[]{:S(2)}, u32[]{:S(2)}) collective-permute-start(f32[384,768]{1,0:T(8,128)S(1)} %collective-permute-done.55), channel_id=1, source_target_pairs={{7,3},{23,19}} | collective-permute-start | bytes 3538952 | tf_op jit(solution)/shard_map/ppermute | solution.py:132
  322.0 24.6 %collective-permute-start.46 = (f32[384,768]{1,0:T(8,128)S(1)}, f32[384,768]{1,0:T(8,128)}, u32[]{:S(2)}, u32[]{:S(2)}) collective-permute-start(f32[384,768]{1,0:T(8,128)S(1)} %collective-permute-done.45), channel_id=1, source_target_pairs={{4,8},{9,13},{20,24},{25,29}} | collective-permute-start | bytes 3538952 | tf_op jit(solution)/shard_map/ppermute | solution.py:132
  333.9 14.4 %collective-permute-start.49 = (f32[384,768]{1,0:T(8,128)S(1)}, f32[384,768]{1,0:T(8,128)}, u32[]{:S(2)}, u32[]{:S(2)}) collective-permute-start(f32[384,768]{1,0:T(8,128)S(1)} %collective-permute-done.48), channel_id=1, source_target_pairs={{6,2},{11,7},{22,18},{27,23}} | collective-permute-start | bytes 3538952 | tf_op jit(solution)/shard_map/ppermute | solution.py:132
  335.6 14.4 %collective-permute-start.40 = (f32[384,768]{1,0:T(8,128)S(1)}, f32[384,768]{1,0:T(8,128)S(1)}, u32[]{:S(2)}, u32[]{:S(2)}) collective-permute-start(f32[384,768]{1,0:T(8,128)S(1)} %collective-permute-done.39), channel_id=1, source_target_pairs={{4,8},{9,13},{20,24},{25,29}} | collective-permute-start | bytes 3538952 | tf_op jit(solution)/shard_map/ppermute | solution.py:132
  336.3 18.7 %collective-permute-start.33 = (f32[384,768]{1,0:T(8,128)S(1)}, f32[384,768]{1,0:T(8,128)}, u32[]{:S(2)}, u32[]{:S(2)}) collective-permute-start(f32[384,768]{1,0:T(8,128)S(1)} %collective-permute-done.32), channel_id=1, source_target_pairs={{0,4},{5,9},{10,14},{16,20},{21,25},{26,30}} | collective-permute-start | bytes 3538952 | tf_op jit(solution)/shard_map/ppermute | solution.py:132
  342.4 14.3 %collective-permute-start.36 = (f32[384,768]{1,0:T(8,128)S(1)}, f32[384,768]{1,0:T(8,128)}, u32[]{:S(2)}, u32[]{:S(2)}) collective-permute-start(f32[384,768]{1,0:T(8,128)S(1)} %collective-permute-done.32), channel_id=1, source_target_pairs={{5,1},{10,6},{15,11},{21,17},{26,22},{31,27}} | collective-permute-start | bytes 3538952 | tf_op jit(solution)/shard_map/ppermute | solution.py:132
  346.6 35.8 %collective-permute-start.43 = (f32[384,768]{1,0:T(8,128)}, f32[384,768]{1,0:T(8,128)}, u32[]{:S(2)}, u32[]{:S(2)}) collective-permute-start(f32[384,768]{1,0:T(8,128)} %collective-permute-done.42), channel_id=1, source_target_pairs={{6,2},{11,7},{22,18},{27,23}} | collective-permute-start | bytes 3538952 | tf_op jit(solution)/shard_map/ppermute | solution.py:132
  348.3 35.8 %collective-permute-start.47 = (f32[384,768]{1,0:T(8,128)}, f32[384,768]{1,0:T(8,128)}, u32[]{:S(2)}, u32[]{:S(2)}) collective-permute-start(f32[384,768]{1,0:T(8,128)} %collective-permute-done.46), channel_id=1, source_target_pairs={{8,12},{24,28}} | collective-permute-start | bytes 3538952 | tf_op jit(solution)/shard_map/ppermute | solution.py:132
  350.0 39.2 %collective-permute-start.50 = (f32[384,768]{1,0:T(8,128)}, f32[384,768]{1,0:T(8,128)}, u32[]{:S(2)}, u32[]{:S(2)}) collective-permute-start(f32[384,768]{1,0:T(8,128)} %collective-permute-done.49), channel_id=1, source_target_pairs={{7,3},{23,19}} | collective-permute-start | bytes 3538952 | tf_op jit(solution)/shard_map/ppermute | solution.py:132
  355.0 30.8 %collective-permute-start.34 = (f32[384,768]{1,0:T(8,128)}, f32[384,768]{1,0:T(8,128)}, u32[]{:S(2)}, u32[]{:S(2)}) collective-permute-start(f32[384,768]{1,0:T(8,128)} %collective-permute-done.33), channel_id=1, source_target_pairs={{4,8},{9,13},{20,24},{25,29}} | collective-permute-start | bytes 3538952 | tf_op jit(solution)/shard_map/ppermute | solution.py:132
  356.8 30.8 %collective-permute-start.37 = (f32[384,768]{1,0:T(8,128)}, f32[384,768]{1,0:T(8,128)}, u32[]{:S(2)}, u32[]{:S(2)}) collective-permute-start(f32[384,768]{1,0:T(8,128)} %collective-permute-done.36), channel_id=1, source_target_pairs={{6,2},{11,7},{22,18},{27,23}} | collective-permute-start | bytes 3538952 | tf_op jit(solution)/shard_map/ppermute | solution.py:132
  382.4 34.1 %collective-permute-start.41 = (f32[384,768]{1,0:T(8,128)}, f32[384,768]{1,0:T(8,128)}, u32[]{:S(2)}, u32[]{:S(2)}) collective-permute-start(f32[384,768]{1,0:T(8,128)} %copy-done.7), channel_id=1, source_target_pairs={{8,12},{24,28}} | collective-permute-start | bytes 3538952 | tf_op jit(solution)/shard_map/ppermute | solution.py:132
  384.1 32.4 %collective-permute-start.44 = (f32[384,768]{1,0:T(8,128)}, f32[384,768]{1,0:T(8,128)}, u32[]{:S(2)}, u32[]{:S(2)}) collective-permute-start(f32[384,768]{1,0:T(8,128)} %collective-permute-done.43), channel_id=1, source_target_pairs={{7,3},{23,19}} | collective-permute-start | bytes 3538952 | tf_op jit(solution)/shard_map/ppermute | solution.py:132
  385.8 57.7 %collective-permute-start.35 = (f32[384,768]{1,0:T(8,128)}, f32[384,768]{1,0:T(8,128)}, u32[]{:S(2)}, u32[]{:S(2)}) collective-permute-start(f32[384,768]{1,0:T(8,128)} %collective-permute-done.34), channel_id=1, source_target_pairs={{8,12},{24,28}} | collective-permute-start | bytes 3538952 | tf_op jit(solution)/shard_map/ppermute | solution.py:132
  387.5 56.0 %collective-permute-start.38 = (f32[384,768]{1,0:T(8,128)}, f32[384,768]{1,0:T(8,128)}, u32[]{:S(2)}, u32[]{:S(2)}) collective-permute-start(f32[384,768]{1,0:T(8,128)} %collective-permute-done.37), channel_id=1, source_target_pairs={{7,3},{23,19}} | collective-permute-start | bytes 3538952 | tf_op jit(solution)/shard_map/ppermute | solution.py:132
  472.6 10.8 %collective-permute-start.58 = (f32[384,768]{1,0:T(8,128)S(1)}, f32[384,768]{1,0:T(8,128)S(1)}, u32[]{:S(2)}, u32[]{:S(2)}) collective-permute-start(f32[384,768]{1,0:T(8,128)S(1)} %get-tuple-element.6), channel_id=1, source_target_pairs={{0,1},{1,0},{2,3},{3,2},{4,5},{5,4},{6,7},{7,6},{8,9},{9,8},{10,11... | collective-permute-start | bytes 3538952 | tf_op jit(solution)/shard_map/ppermute | solution.py:96
  480.9 18.4 %collective-permute-start.57 = (f32[384,768]{1,0:T(8,128)S(1)}, f32[384,768]{1,0:T(8,128)S(1)}, u32[]{:S(2)}, u32[]{:S(2)}) collective-permute-start(f32[384,768]{1,0:T(8,128)S(1)} %get-tuple-element.5), channel_id=1, source_target_pairs={{0,1},{1,0},{2,3},{3,2},{4,5},{5,4},{6,7},{7,6},{8,9},{9,8},{10,11... | collective-permute-start | bytes 3538952 | tf_op jit(solution)/shard_map/ppermute | solution.py:96
  483.6 42.0 %collective-permute-start.59 = (f32[384,768]{1,0:T(8,128)S(1)}, f32[384,768]{1,0:T(8,128)S(1)}, u32[]{:S(2)}, u32[]{:S(2)}) collective-permute-start(f32[384,768]{1,0:T(8,128)S(1)} %slice_add_fusion), channel_id=1, source_target_pairs={{0,2},{1,3},{2,0},{3,1},{4,6},{5,7},{6,4},{7,5},{8,10},{9,11},{10,... | collective-permute-start | bytes 3538952 | tf_op jit(solution)/shard_map/ppermute | solution.py:96
  (19 other events, 306.4 us)
